TPU v7x, 256 devices: a whole 4x4x8 slice. The times are simulated.
256 devices in a mesh: span: 4 (over y), blk: 16 (over z, x_lo), head: 4 (over x_hi, core).
Axes of the slice: x: 4 (x_hi: 2, x_lo: 2; x = x_hi * 2 + x_lo), y: 4, z: 8, core: 2. Of those that a mesh axis runs over, the one named last changes fastest.
Arguments:
- queries: bfloat16 [4, 1536, 4096], P('span', ('blk', 'head')), may hold values from -8 to 8
- keys: bfloat16 [4, 1536, 4096], P('span', ('blk', 'head')), may hold values from -8 to 8
- values: bfloat16 [4, 1536, 4096], P('span', ('blk', 'head')), may hold values from -6 to 6
- stream: bfloat16 [4, 1536, 6144], P('span', ('blk', 'head')), may hold values from -6 to 6
- latent: float32 [4, 1536, 64], P('span', ('blk', 'head')), may hold values from -6 to 6
- w_out: bfloat16 [4096, 6144], P('head'), may hold values from -0.09375 to 0.09375
- w_velocity: bfloat16 [6144, 64], replicated, may hold values from -0.078125 to 0.078125
- noise_level: int32 [4], replicated, may hold values from 0 to 7
- valid_len: int32 [4], replicated, may hold values from 768 to 1536, as said below
- span_mask: int32 [4, 4], replicated, may hold values from 0 to 1, as said below
Outputs:
- stream_out: bfloat16 [4, 1536, 6144], P('span', ('blk', 'head'))
- latent_next: float32 [4, 1536, 64], P('span', ('blk', 'head'))
Inputs may be any that keep to these rules, and one draw needn't show every extreme that they name: `valid_len`: at least half of each span's tokens are valid; some span is whole in every draw. span_mask[c, c] = 1 and span_mask[c, c2] = 0 for c2 > c.
All inputs are finite; a program needn't handle non-finite values.
Results may differ from a plain program's by a relative error of at most 0.008.
Values may be sent and summed in bfloat16 or wider, within the bound.
A program may use at most 128 MiB of HBM per device.

v0:
```python
import jax
import jax.numpy as jnp
from jax import lax
from jax.sharding import PartitionSpec as P

HD = 128
LEVELS = 8


def sigma_of(level):
    u = 1.0 - level.astype(jnp.float32) / LEVELS
    return 3.0 * u / (1.0 + 2.0 * u)


def attend(carry, key_rows, val_rows, span_ids, positions, query_heads, allow_row, valid_len):
    best, total, summed = carry
    count = key_rows.shape[0]
    heads = query_heads.shape[1]
    key_heads = key_rows.reshape(count, heads, HD)
    val_heads = val_rows.reshape(count, heads, HD)
    scores = jnp.einsum(
        "qhd,khd->hqk", query_heads, key_heads, preferred_element_type=jnp.float32
    ) * HD ** (-0.5)
    member = span_ids[:, None] == jnp.arange(allow_row.shape[0], dtype=jnp.int32)[None, :]
    permitted = jnp.sum(jnp.where(member, allow_row[None, :], 0), axis=1) == 1
    limit = jnp.sum(jnp.where(member, valid_len[None, :], 0), axis=1)
    keep = permitted & (positions < limit)
    masked = jnp.where(keep[None, None, :], scores, -1e30)
    fresh = jnp.maximum(best, jnp.max(masked, axis=2))
    unnorm = jnp.where(keep[None, None, :], jnp.exp(masked - fresh[:, :, None]), 0.0)
    total = jnp.sum(unnorm, axis=2)
    summed = jnp.einsum(
        "hqk,khd->hqd", unnorm.astype(jnp.bfloat16), val_heads, preferred_element_type=jnp.float32
    )
    return (fresh, total, summed)


def on_device(
    queries, keys, values, stream, latent, w_out, w_velocity, noise_level, valid_len, span_mask
):
    mine_q, mine_k, mine_v = (
        lax.all_to_all(queries, "head", split_axis=2, concat_axis=1, tiled=True),
        lax.all_to_all(keys, "head", split_axis=2, concat_axis=1, tiled=True),
        lax.all_to_all(values, "head", split_axis=2, concat_axis=1, tiled=True),
    )
    rows = mine_q.shape[1]
    feats = mine_q.shape[2]
    heads = feats // HD
    query_heads = mine_q[0].reshape(rows, heads, HD)
    my_span = lax.axis_index("span")
    allow_row = span_mask[my_span]
    init = (
        jnp.full((heads, rows), -1e30, jnp.float32),
        jnp.zeros((heads, rows), jnp.float32),
        jnp.zeros((heads, rows, HD), jnp.float32),
    )
    every_k, every_v = (
        lax.all_gather(mine_k, "span", axis=0, tiled=True),
        lax.all_gather(mine_v, "span", axis=0, tiled=True),
    )
    spans = every_k.shape[0]
    pieces = (
        lax.all_gather(every_k, "blk", axis=1, tiled=True),
        lax.all_gather(every_v, "blk", axis=1, tiled=True),
    )
    count = pieces[0].shape[1]
    span_ids = jnp.repeat(jnp.arange(spans, dtype=jnp.int32), count)
    positions = jnp.tile(jnp.arange(count, dtype=jnp.int32), spans)
    best, total, summed = attend(
        init,
        pieces[0].reshape(spans * count, feats),
        pieces[1].reshape(spans * count, feats),
        span_ids,
        positions,
        query_heads,
        allow_row,
        valid_len,
    )
    attn = (
        jnp.transpose(summed / total[:, :, None], (1, 0, 2))
        .reshape(rows, feats)
        .astype(jnp.bfloat16)
    )
    update = lax.psum_scatter(
        jnp.dot(attn, w_out, preferred_element_type=jnp.float32).astype(jnp.bfloat16),
        "head",
        scatter_dimension=0,
        tiled=True,
    ).astype(jnp.float32)
    stream_out = (stream[0].astype(jnp.float32) + update).astype(jnp.bfloat16)
    velocity = jnp.dot(stream_out, w_velocity, preferred_element_type=jnp.float32)
    level = noise_level[my_span]
    step = sigma_of(level + 1) - sigma_of(level)
    latent_next = latent[0] + step * velocity
    return (stream_out[None], latent_next[None])


def solution(mesh):
    return jax.shard_map(
        on_device,
        mesh=mesh,
        in_specs=(
            P("span", ("blk", "head"), None),
            P("span", ("blk", "head"), None),
            P("span", ("blk", "head"), None),
            P("span", ("blk", "head"), None),
            P("span", ("blk", "head"), None),
            P("head", None),
            P(),
            P(),
            P(),
            P(),
        ),
        out_specs=(P("span", ("blk", "head"), None), P("span", ("blk", "head"), None)),
        check_vma=False,
    )
```

profile of v0, /device:TPU:25, one launch (start us, length us, event | category | flops | bytes accessed | tf_op | source)
XLA Modules:
  0.0 707.3 jit_solution(11893062135948152020)
XLA Ops:
  7.2 4.5 copy.52
  12.3 23.4 %reduce.1 = bf16[4096,24]{1,0:T(8,128)(2,1)} reduce(bf16[4096,1,24]{2,1,0:T(2,128)(2,1)S(1)} %bitcast.56, bf16[]{:T(256)} %broadcast.10), dimensions={1}, to_apply=%bitcast.46.reduce_sub_computation | reduce | bytes 393218
  35.7 2.5 reshape.56
  38.3 10.9 %all_to_all.51 = bf16[4,2,12288]{2,1,0:T(2,128)(2,1)S(1)} all-to-all(bf16[4,2,12288]{2,1,0:T(2,128)(2,1)S(1)} %reshape.56), channel_id=1, replica_groups=mesh['span'=4,'blk'=16,'head'=4] {'head'}, dimensions={0} | all-to-all | bytes 393216 | tf_op jit(solution)/shard_map/all_to_all | solution.py:43
  49.1 2.8 reshape.57
  51.9 2.1 copy.53
  54.2 11.2 %all_gather.12 = bf16[4,96,1024]{2,1,0:T(8,128)(2,1)} all-gather(bf16[1,96,1024]{2,1,0:T(8,128)(2,1)S(1)} %bitcast.67), channel_id=1, replica_groups=mesh['span'=4,'blk'=16,'head'=4] {'span'}, dimensions={0}, use_global_device_ids=true | all-gather | bytes 983040 | tf_op jit(solution)/shard_map/all_gather | solution.py:58
  65.8 2.8 copy.57
  68.5 23.5 %reduce = bf16[4096,24]{1,0:T(8,128)(2,1)} reduce(bf16[4096,1,24]{2,1,0:T(2,128)(2,1)S(1)} %bitcast.61, bf16[]{:T(256)} %broadcast.10), dimensions={1}, to_apply=%bitcast.44.reduce_sub_computation | reduce | bytes 393218
  92.0 2.5 reshape.54
  94.6 16.3 %all_to_all.52 = bf16[4,2,12288]{2,1,0:T(2,128)(2,1)S(1)} all-to-all(bf16[4,2,12288]{2,1,0:T(2,128)(2,1)S(1)} %reshape.54), channel_id=1, replica_groups=mesh['span'=4,'blk'=16,'head'=4] {'head'}, dimensions={0} | all-to-all | bytes 393216 | tf_op jit(solution)/shard_map/all_to_all | solution.py:44
  110.9 2.8 reshape.55
  113.7 2.1 copy.58
  116.0 12.7 %all_gather.14 = bf16[4,96,1024]{2,1,0:T(8,128)(2,1)} all-gather(bf16[1,96,1024]{2,1,0:T(8,128)(2,1)S(1)} %bitcast.68), channel_id=1, replica_groups=mesh['span'=4,'blk'=16,'head'=4] {'span'}, dimensions={0}, use_global_device_ids=true | all-gather | bytes 983040 | tf_op jit(solution)/shard_map/all_gather | solution.py:59
  128.7 2.8 copy.49
  131.5 23.5 %reduce.2 = bf16[4096,24]{1,0:T(8,128)(2,1)} reduce(bf16[4096,1,24]{2,1,0:T(2,128)(2,1)S(1)} %bitcast.59, bf16[]{:T(256)} %broadcast.10), dimensions={1}, to_apply=%bitcast.48.reduce_sub_computation | reduce | bytes 393218
  154.9 3.2 reshape.58
  158.2 6.5 all-to-all-start
  165.9 12.3 %all-to-all-done = bf16[4,2,12288]{2,1,0:T(2,128)(2,1)S(1)} async-done(((bf16[4,2,12288]{2,1,0:T(2,128)(2,1)}), bf16[4,2,12288]{2,1,0:T(2,128)(2,1)S(1)}, u32[]{:S(2)}, u32[]{:S(2)}) %all-to-all-start) | async-done | bytes 196640 | tf_op jit(solution)/shard_map/all_to_all | solution.py:42
  178.2 2.8 reshape.59
  181.0 2.1 copy.50
  183.4 156.9 %all-gather.3.cloned.1.call-done = bf16[4,1536,1024]{2,1,0:T(8,128)(2,1)} async-done(((bf16[4,96,1024]{2,1,0:T(8,128)(2,1)}), bf16[4,1536,1024]{2,1,0:T(8,128)(2,1)}) %all-gather.3.cloned.1.call-update) | async-done | bytes 12582928 | tf_op jit(solution)/shard_map/all_gather | solution.py:63
  340.3 11.9 %copy.64 = bf16[768,8,8,128]{3,2,1,0:T(8,128)(2,1)} copy(bf16[768,8,8,128]{3,1,2,0:T(8,128)(2,1)} %bitcast.53) | data formatting | bytes 25165824
  352.2 13.7 %fusion = (f32[8,96]{1,0:T(8,128)S(1)}, f32[8,96,6144]{2,1,0:T(8,128)}) fusion(pred[6144]{0:T(1024)(128)(4,1)S(1)} %compare_and_fusion, bf16[6144,8,128]{2,1,0:T(8,128)(2,1)} %bitcast.52, bf16[96,8,128]{2,1,0:T(8,128)(2,1)S(1)} %bitcast.62), kind=kOutput, calls=%fused_computation.2 | convolution fusion | flops 1222114560 | bytes 31663104 | tf_op jit(solution)/shard_map/qhd,khd->hqk/dot_general | solution.py:21
  365.9 245.3 %all-gather.5.cloned.1.call-done = bf16[4,1536,1024]{2,1,0:T(8,128)(2,1)} async-done(((bf16[4,96,1024]{2,1,0:T(8,128)(2,1)}), bf16[4,1536,1024]{2,1,0:T(8,128)(2,1)}) %all-gather.5.cloned.1.call-update) | async-done | bytes 12582928 | tf_op jit(solution)/shard_map/all_gather | solution.py:64
  611.1 11.9 %copy.65 = bf16[768,8,8,128]{3,2,1,0:T(8,128)(2,1)} copy(bf16[768,8,8,128]{3,1,2,0:T(8,128)(2,1)} %bitcast.54) | data formatting | bytes 25165824
  623.0 11.6 %fusion.1 = f32[8,96]{1,0:T(8,128)S(1)} fusion(f32[8,96,6144]{2,1,0:T(8,128)} %get-tuple-element.5, f32[8,96]{1,0:T(8,128)S(1)} %broadcast_maximum_fusion, pred[6144]{0:T(1024)(128)(4,1)S(1)} %compare_and_fusion), kind=kLoop, calls=%fused_computation.3 | loop fusion | flops 23592192 | bytes 18886656 | tf_op jit(solution)/shard_map/reduce_sum | solution.py:31
  634.6 14.1 %fusion.28 = bf16[8,12,8,128]{3,2,1,0:T(8,128)(2,1)S(1)} fusion(bf16[6144,8,128]{2,1,0:T(8,128)(2,1)} %bitcast.55, f32[8,96,6144]{2,1,0:T(8,128)} %get-tuple-element.5, f32[8,96]{1,0:T(8,128)S(1)} %broadcast_maximum_fusion, pred[6144]{0:T(1024)(128)(4,1)S(1)} %compare_and_fusion, f32[96,8]{0,1:T(8,128)S(1)} %bitcast.69), kind=kOutput, calls=%fused_computation.18 | convolution fusion | flops 1231749120 | bytes 31666176 | tf_op jit(solution)/shard_map/hqk,khd->hqd/dot_general | solution.py:32
  648.7 7.7 %convolution_convert_fusion = bf16[96,6144]{1,0:T(8,128)(2,1)} fusion(bf16[1024,6144]{1,0:T(8,128)(2,1)} %param.15, bf16[8,12,8,128]{3,2,1,0:T(8,128)(2,1)S(1)} %fusion.28), kind=kOutput, calls=%fused_computation.14 | convolution fusion | flops 1208549376 | bytes 13959168 | tf_op jit(solution)/shard_map/dot_general | solution.py:85
  658.4 38.4 %reduce-scatter.2.cloned.1.call-done = bf16[24,6144]{1,0:T(8,128)(2,1)} async-done(((bf16[96,6144]{1,0:T(8,128)(2,1)}), bf16[24,6144]{1,0:T(8,128)(2,1)}) %reduce-scatter.2.cloned.1.call-update) | async-done | bytes 294928 | tf_op jit(solution)/shard_map/reduce_scatter | solution.py:84
  696.9 1.7 fusion.40
  698.6 1.9 fusion.34
  (37 shorter events, 3.3 us)
Async XLA Ops:
  7.2 691.5 %copy-start = (bf16[6144,64]{0,1:T(8,128)(2,1)S(1)}, bf16[6144,64]{0,1:T(8,128)(2,1)}, u32[]{:S(2)}) copy-start(bf16[6144,64]{0,1:T(8,128)(2,1)} %param.16) | copy-start | bytes 2359300
  7.2 58.6 %copy-start.2 = (bf16[1,24,4096]{2,1,0:T(8,128)(2,1)S(1)}, bf16[1,24,4096]{2,1,0:T(8,128)(2,1)}, u32[]{:S(2)}) copy-start(bf16[1,24,4096]{2,1,0:T(8,128)(2,1)} %param.12) | copy-start | bytes 589828
  7.2 333.1 %all-gather.3.cloned.1.call-start = ((), (), s32[]{:S(2)}) async-start(), calls=%async_computation.4 | async-start | bytes 13369344 | tf_op jit(solution)/shard_map/all_gather | solution.py:63
  12.2 116.4 %copy-start.3 = (bf16[1,24,4096]{2,1,0:T(8,128)(2,1)S(1)}, bf16[1,24,4096]{2,1,0:T(8,128)(2,1)}, u32[]{:S(2)}) copy-start(bf16[1,24,4096]{2,1,0:T(8,128)(2,1)} %param.10) | copy-start | bytes 589828
  54.0 111.6 %copy-start.5 = (s32[4]{0:T(128)S(1)}, s32[4]{0:T(128)}, u32[]{:S(2)}) copy-start(s32[4]{0:T(128)} %param.18) | copy-start | bytes 52
  65.4 545.7 %all-gather.5.cloned.1.call-start = ((), (), s32[]{:S(2)}) async-start(), calls=%async_computation.5 | async-start | bytes 13369344 | tf_op jit(solution)/shard_map/all_gather | solution.py:64
  158.2 20.0 %all-to-all-start = ((bf16[4,2,12288]{2,1,0:T(2,128)(2,1)}), bf16[4,2,12288]{2,1,0:T(2,128)(2,1)S(1)}, u32[]{:S(2)}, u32[]{:S(2)}) async-start(bf16[4,2,12288]{2,1,0:T(2,128)(2,1)} %reshape.58), calls=%async_computation | async-start | bytes 393216 | tf_op jit(solution)/shard_map/all_to_all | solution.py:42
  164.7 532.2 %reduce-scatter.2.cloned.1.call-start = ((), (), s32[]{:S(2)}) async-start(), calls=%async_computation.6 | async-start | bytes 1474560 | tf_op jit(solution)/shard_map/reduce_scatter | solution.py:84
  648.7 7.8 %copy-start.6 = (s32[4]{0:T(128)S(1)}, s32[4]{0:T(128)}, u32[]{:S(2)}) copy-start(s32[4]{0:T(128)} %param.17) | copy-start | bytes 52
  648.7 48.2 %copy-start.1 = (bf16[1,24,6144]{2,1,0:T(8,128)(2,1)S(1)}, bf16[1,24,6144]{2,1,0:T(8,128)(2,1)}, u32[]{:S(2)}) copy-start(bf16[1,24,6144]{2,1,0:T(8,128)(2,1)} %param.13) | copy-start | bytes 884740
  648.7 50.0 %copy-start.4 = (f32[1,24,64]{2,1,0:T(8,128)S(1)}, f32[1,24,64]{2,1,0:T(8,128)}, u32[]{:S(2)}) copy-start(f32[1,24,64]{2,1,0:T(8,128)} %param.14) | copy-start | bytes 18436
Sparse Core Ops, SparseCore 0:
  65.6 274.6 all-gather.2
  342.1 269.0 all-gather.4
  656.6 40.2 reduce-scatter.1
where the time goes:
time: 715 us; the launch traced here: 707 us
  waiting for transfers between devices  453 us (63%)
  other arithmetic  83.9 us (12%)
  local copies, waits for them, and re-layouts  59.3 us (8%)
  blocking collectives  51 us (7%)
  matrix products  37.4 us (5%)
  between operations  15.6 us (2%)
    all_gather x1, waiting for transfers between devices, on_device(): lax.all_gather(every_v, 'blk', axis=1, tiled=True)  245 us
    all_gather x1, waiting for transfers between devices, on_device(): lax.all_gather(every_k, 'blk', axis=1, tiled=True)  157 us
    unnamed x3, other arithmetic  70.4 us
    unnamed x27, local copies, waits for them, and re-layouts  51 us
    reduce_scatter x1, waiting for transfers between devices, on_device(): lax.psum_scatter(jnp.dot(attn, w_out, preferred_element_type=jnp.float32)...  38.4 us
    all_to_all x1, blocking collectives, on_device(): lax.all_to_all(values, 'head', split_axis=2, concat_axis=1, tiled=True)  16.3 us
  transfers between devices with their start and end apart: 4, of which 4 were waited for; matrix products, arithmetic and copies ran while one was open for 13% of the time, Pallas kernels for 0%

commit v1 on v0

v1 whole, which is shorter than its diff:
```python
import functools

import jax
import jax.numpy as jnp
from jax import lax
from jax.experimental import pallas as pl
from jax.experimental.pallas import tpu as pltpu
from jax.sharding import PartitionSpec as P

HD = 128
LEVELS = 8
SPANS = 4
BLKS = 16
ROWS = 24
HEADS = 32
SLOTS = 32
TOK = SLOTS * ROWS
MODEL = 6144
GROUP = 1024
CHUNKS = 6
WIDE = MODEL // CHUNKS
SCALE = HD ** -0.5
NEG = -1e30
MESH = pl.DeviceIdType.MESH
BF = jnp.bfloat16
F32 = jnp.float32


def place():
    span = lax.axis_index("span")
    blk = lax.axis_index("blk")
    head = lax.axis_index("head")
    return span, blk, lax.div(head, 2), lax.rem(head, 2)


def flip(blk):
    return blk + 1 - 2 * lax.rem(blk, 2)


def gather_kernel(
    q_ref, k_ref, v_ref, qo_ref, kv_ref, packq, packkv, a_send, a_recv, a_own,
    y_send, y_recv, c_send, c_recv,
):
    span, blk, half, core = place()
    mine = half * BLKS + blk
    sibling = {"head": half * 2 + 1 - core}
    barrier = pltpu.get_barrier_semaphore()

    def greet(i, carry):
        other = lax.rem(mine + i, HEADS)
        pl.semaphore_signal(
            barrier, inc=1, device_id={"blk": lax.rem(other, BLKS), "head": lax.div(other, BLKS) * 2 + core},
            device_id_type=MESH,
        )
        return carry

    lax.fori_loop(1, HEADS, greet, 0)
    pl.semaphore_signal(barrier, inc=1, device_id=sibling, device_id_type=MESH)
    for i in range(1, SPANS):
        pl.semaphore_signal(barrier, inc=1, device_id={"span": lax.rem(span + i, SPANS)}, device_id_type=MESH)

    for h in range(HEADS):
        cols = slice(h * HD, (h + 1) * HD)
        packkv[h, 0] = k_ref[0, :, cols]
        packkv[h, 1] = v_ref[0, :, cols]
        packq[h] = q_ref[0, :, cols]

    pl.semaphore_wait(barrier, HEADS - 1 + 1 + SPANS - 1)

    def target(i):
        other = lax.rem(mine + i, HEADS)
        there = lax.div(other, BLKS)
        cross = lax.rem(half + there, 2)
        slot = blk + cross * (1 - 2 * lax.rem(blk, 2))
        return other, {"blk": lax.rem(other, BLKS), "head": there * 2 + core}, slot, cross

    def send_kv(i, carry):
        other, device, slot, cross = target(i)
        pltpu.make_async_remote_copy(
            packkv.at[other], kv_ref.at[span, 0, slot, cross], a_send.at[0], a_recv.at[0],
            device_id=device, device_id_type=MESH,
        ).start()
        return carry

    def send_q(i, carry):
        other, device, slot, cross = target(i)
        pltpu.make_async_remote_copy(
            packq.at[other], qo_ref.at[slot, cross], a_send.at[1], a_recv.at[1],
            device_id=device, device_id_type=MESH,
        ).start()
        return carry

    lax.fori_loop(1, HEADS, send_kv, 0)
    own_kv = pltpu.make_async_copy(packkv.at[mine], kv_ref.at[span, 0, blk, 0], a_own.at[0])
    own_q = pltpu.make_async_copy(packq.at[mine], qo_ref.at[blk, 0], a_own.at[1])
    own_kv.start()
    own_q.start()
    lax.fori_loop(1, HEADS, send_q, 0)
    own_kv.wait()

    def all_kv(sem):
        pltpu.make_async_copy(packkv.at[pl.ds(0, HEADS - 1)], packkv.at[pl.ds(0, HEADS - 1)], sem).wait()

    def all_q(sem):
        pltpu.make_async_copy(packq.at[pl.ds(0, HEADS - 1)], packq.at[pl.ds(0, HEADS - 1)], sem).wait()

    all_kv(a_recv.at[0])

    def piece(c2, p, rel=0):
        return kv_ref.at[c2, rel, pl.ds(p * 8, 8)]

    def along(c2, p, to, which):
        return pltpu.make_async_remote_copy(
            piece(c2, p), piece(c2, p), y_send.at[which], y_recv.at[c2, p],
            device_id={"span": to}, device_id_type=MESH,
        )

    def beside(c2, p):
        return pltpu.make_async_remote_copy(
            piece(c2, p), piece(c2, p, 1), c_send.at[c2, p], c_recv.at[c2, p],
            device_id=sibling, device_id_type=MESH,
        )

    @pl.when(span == 0)
    def _():
        sends = [along(0, 0, 1, 0), along(0, 1, 3, 1), along(0, 1, 1, 2), along(0, 0, 3, 3)]
        for s in sends:
            s.start()
        over = [beside(0, 0), beside(0, 1)]
        for s in over:
            s.start()
        relay = along(1, 1, 3, 4)
        relay.wait_recv()
        relay.start()
        for s in sends + [relay]:
            s.wait_send()
        for s in over:
            s.wait()

    @pl.when(span == 1)
    def _():
        sends = [along(1, 1, 0, 0), along(1, 0, 2, 1), along(1, 1, 2, 2)]
        for s in sends:
            s.start()
        over = [beside(1, 0), beside(1, 1), beside(0, 0), beside(0, 1)]
        over[0].start()
        over[1].start()
        relay = along(0, 0, 2, 3)
        relay.wait_recv()
        relay.start()
        over[2].start()
        along(0, 1, 2, 4).wait_recv()
        over[3].start()
        for s in sends + [relay]:
            s.wait_send()
        for s in over:
            s.wait()

    @pl.when(span == 2)
    def _():
        sends = [along(2, 0, 3, 0), along(2, 1, 3, 1)]
        for s in sends:
            s.start()
        over = [beside(2, 0), beside(2, 1)]
        for s in over:
            s.start()
        relay = along(1, 0, 3, 2)
        relay.wait_recv()
        relay.start()
        for c2, p in ((1, 0), (1, 1), (0, 0), (0, 1)):
            if (c2, p) != (1, 0):
                along(c2, p, 3, 3).wait_recv()
            s = beside(c2, p)
            s.start()
            over.append(s)
        for s in sends + [relay]:
            s.wait_send()
        for s in over:
            s.wait()

    @pl.when(span == 3)
    def _():
        over = [beside(3, 0), beside(3, 1)]
        for s in over:
            s.start()
        relay = along(0, 1, 2, 0)
        relay.wait_recv()
        relay.start()
        for c2, p in ((0, 1), (2, 0), (0, 0), (2, 1), (1, 0), (1, 1)):
            if (c2, p) != (0, 1):
                along(c2, p, 2, 1).wait_recv()
            s = beside(c2, p)
            s.start()
            over.append(s)
        relay.wait_send()
        for s in over:
            s.wait()

    all_q(a_recv.at[1])
    all_kv(a_send.at[0])
    all_q(a_send.at[1])
    own_q.wait()


def gather(queries, keys, values):
    vm = pl.BlockSpec(memory_space=pltpu.VMEM)
    return pl.pallas_call(
        gather_kernel,
        out_shape=(
            jax.ShapeDtypeStruct((BLKS, 2, ROWS, HD), BF),
            jax.ShapeDtypeStruct((SPANS, 2, BLKS, 2, 2, ROWS, HD), BF),
        ),
        in_specs=[vm] * 3,
        out_specs=(vm, vm),
        scratch_shapes=[
            pltpu.VMEM((HEADS, ROWS, HD), BF),
            pltpu.VMEM((HEADS, 2, ROWS, HD), BF),
            pltpu.SemaphoreType.DMA((2,)),
            pltpu.SemaphoreType.DMA((2,)),
            pltpu.SemaphoreType.DMA((2,)),
            pltpu.SemaphoreType.DMA((5,)),
            pltpu.SemaphoreType.DMA((4, 2)),
            pltpu.SemaphoreType.DMA((4, 2)),
            pltpu.SemaphoreType.DMA((4, 2)),
        ],
        compiler_params=pltpu.CompilerParams(
            collective_id=0, has_side_effects=True, vmem_limit_bytes=32 * 2**20
        ),
        name="gather",
    )(queries, keys, values)


def attend_kernel(mask_ref, valid_ref, q_ref, kv_ref, o_ref, qx, kx, vx, acc, best):
    span, blk, half, core = place()
    lane = lax.broadcasted_iota(jnp.int32, (TOK, HD), 1)
    first = lane == 0
    qx[:, :HD] = q_ref[...].reshape(TOK, HD)
    qx[:, HD:] = jnp.where(first, 1.0, 0.0).astype(BF)
    acc[...] = jnp.zeros_like(acc)
    best[...] = jnp.full_like(best, NEG)
    row = lax.broadcasted_iota(jnp.int32, (TOK, HD), 0)
    slot = lax.div(row, 2 * ROWS)
    inner = lax.rem(row, 2 * ROWS)
    cross = (inner >= ROWS).astype(jnp.int32)
    sblk = slot + cross * (1 - 2 * lax.rem(slot, 2))
    shalf = lax.rem(half + cross, 2)
    base = sblk * (4 * ROWS) + shalf * (2 * ROWS) + lax.rem(row, ROWS)
    for rel in range(2):
        vx[rel, :, HD:] = jnp.where(first, 1.0, 0.0).astype(BF)

    def one_span(c2, carry):
        @pl.when(mask_ref[span, c2] == 1)
        def _():
            for rel in range(2):
                kx[rel, :, :HD] = kv_ref[c2, rel, :, :, 0].reshape(TOK, HD)
                vx[rel, :, :HD] = kv_ref[c2, rel, :, :, 1].reshape(TOK, HD)
                pos = base + lax.rem(core + rel, 2) * ROWS
                kx[rel, :, HD:] = jnp.where(first & (pos >= valid_ref[c2]), NEG, 0.0).astype(BF)

            def tile(t, carry):
                rows = pl.ds(pl.multiple_of(t * 256, 256), 256)
                for rel in range(2):
                    scores = lax.dot_general(
                        qx[rows], kx[rel], (((1,), (1,)), ((), ())), preferred_element_type=F32
                    ) * SCALE
                    old = best[rows]
                    fresh = jnp.maximum(old, jnp.max(scores, axis=1, keepdims=True))
                    unnorm = jnp.exp(scores - fresh[:, :1]).astype(BF)
                    part = jnp.dot(unnorm, vx[rel], preferred_element_type=F32)
                    acc[rows] = acc[rows] * jnp.exp(old - fresh)[:, :1] + part
                    best[rows] = fresh
                return carry

            lax.fori_loop(0, TOK // 256, tile, 0)

        return carry

    lax.fori_loop(0, span + 1, one_span, 0)
    o_ref[...] = (acc[:, :HD] / acc[:, HD : HD + 1]).astype(BF).reshape(BLKS, 2, ROWS, HD)


def attention(span_mask, valid_len, q, kv):
    vm = pl.BlockSpec(memory_space=pltpu.VMEM)
    sm = pl.BlockSpec(memory_space=pltpu.SMEM)
    return pl.pallas_call(
        attend_kernel,
        out_shape=jax.ShapeDtypeStruct((BLKS, 2, ROWS, HD), BF),
        in_specs=[sm, sm, vm, vm],
        out_specs=vm,
        scratch_shapes=[
            pltpu.VMEM((TOK, 2 * HD), BF),
            pltpu.VMEM((2, TOK, 2 * HD), BF),
            pltpu.VMEM((2, TOK, 2 * HD), BF),
            pltpu.VMEM((TOK, 2 * HD), F32),
            pltpu.VMEM((TOK, HD), F32),
        ],
        compiler_params=pltpu.CompilerParams(vmem_limit_bytes=40 * 2**20),
        name="attend",
    )(span_mask, valid_len, q, kv)


def project_kernel(
    noise_ref, o_ref, stream_ref, latent_ref, wv_ref, w_hbm, out_ref, next_ref,
    w_buf, heads, lhs, near_out, near_in, far_out, far_in,
    w_sem, h_send, h_recv, h_own, n_send, n_recv, f_send, f_recv,
):
    span, blk, half, core = place()
    loads = [
        pltpu.make_async_copy(w_hbm.at[:, pl.ds(n * WIDE, WIDE)], w_buf.at[n], w_sem.at[n]) for n in range(CHUNKS)
    ]
    for load in loads:
        load.start()
    sibling = {"head": half * 2 + 1 - core}
    partner = {"blk": flip(blk), "head": (1 - half) * 2 + core}
    barrier = pltpu.get_barrier_semaphore()
    me = blk * 2 + core

    def greet(i, carry):
        other = lax.rem(me + i, 2 * BLKS)
        pl.semaphore_signal(
            barrier, inc=1, device_id={"blk": lax.div(other, 2), "head": half * 2 + lax.rem(other, 2)},
            device_id_type=MESH,
        )
        return carry

    lax.fori_loop(1, 2 * BLKS, greet, 0)
    pl.semaphore_signal(barrier, inc=1, device_id=partner, device_id_type=MESH)
    pl.semaphore_wait(barrier, 2 * BLKS)

    goal = lax.div(blk, 8)
    rel = lax.rem(goal + core, 2)
    lane = lax.rem(blk, 8)

    def send(i, carry):
        other = lax.rem(blk + i, BLKS)
        pltpu.make_async_remote_copy(
            o_ref.at[other], heads.at[rel, lane], h_send, h_recv,
            device_id={"blk": other, "head": half * 2 + goal}, device_id_type=MESH,
        ).start()
        return carry

    lax.fori_loop(1, BLKS, send, 0)
    keep = goal == core

    @pl.when(keep)
    def _():
        own = pltpu.make_async_copy(o_ref.at[blk], heads.at[rel, lane], h_own)
        own.start()
        own.wait()
        pltpu.make_async_copy(o_ref.at[pl.ds(0, 15)], o_ref.at[pl.ds(0, 15)], h_recv).wait()
        pltpu.make_async_copy(o_ref.at[pl.ds(0, 15)], o_ref.at[pl.ds(0, 15)], h_send).wait()

    @pl.when(jnp.logical_not(keep))
    def _():
        pltpu.make_async_remote_copy(
            o_ref.at[blk], heads.at[rel, lane], h_send, h_recv,
            device_id={"blk": blk, "head": half * 2 + goal}, device_id_type=MESH,
        ).start()
        pltpu.make_async_copy(o_ref, o_ref, h_recv).wait()
        pltpu.make_async_copy(o_ref, o_ref, h_send).wait()

    @pl.when(True)
    def _():
        for r in range(2):
            for j in range(8):
                lhs[r * 48 : (r + 1) * 48, j * HD : (j + 1) * HD] = heads[r, j].reshape(48, HD)

    def near(n):
        return pltpu.make_async_remote_copy(
            near_out.at[n], near_in.at[n], n_send.at[n], n_recv.at[n], device_id=sibling, device_id_type=MESH
        )

    def far(n):
        return pltpu.make_async_remote_copy(
            far_out.at[n], far_in.at[n], f_send.at[n], f_recv.at[n], device_id=partner, device_id_type=MESH
        )

    held = [None] * CHUNKS
    velocity = jnp.zeros((ROWS, 64), F32)
    for n in range(CHUNKS + 2):
        if n < CHUNKS:
            loads[n].wait()
            part = jnp.dot(lhs[...], w_buf[n], preferred_element_type=F32)
            near_out[n] = part[48:].astype(BF).reshape(2, ROWS, WIDE)
            near(n).start()
            held[n] = part[:48]
        m = n - 1
        if 0 <= m < CHUNKS:
            near(m).wait_recv()
            held[m] = held[m].reshape(2, ROWS, WIDE) + near_in[m].astype(F32)
            far_out[m] = held[m][1].astype(BF)
            far(m).start()
            held[m] = held[m][0]
        m = n - 2
        if 0 <= m < CHUNKS:
            far(m).wait_recv()
            cols = slice(m * WIDE, (m + 1) * WIDE)
            fresh = (stream_ref[0, :, cols].astype(F32) + (held[m] + far_in[m].astype(F32))).astype(BF)
            out_ref[0, :, cols] = fresh
            velocity += lax.dot_general(
                fresh, wv_ref[:, cols], (((1,), (1,)), ((), ())), preferred_element_type=F32
            )
    level = jnp.full((ROWS, 64), noise_ref[span], jnp.int32).astype(F32)

    def sigma(value):
        u = 1.0 - value / LEVELS
        return 3.0 * u / (1.0 + 2.0 * u)

    next_ref[0] = latent_ref[0] + (sigma(level + 1.0) - sigma(level)) * velocity
    for n in range(CHUNKS):
        near(n).wait_send()
        far(n).wait_send()


def project(noise_level, o, stream, latent, w_velocity, w_out):
    vm = pl.BlockSpec(memory_space=pltpu.VMEM)
    sm = pl.BlockSpec(memory_space=pltpu.SMEM)
    return pl.pallas_call(
        project_kernel,
        out_shape=(
            jax.ShapeDtypeStruct((1, ROWS, MODEL), BF),
            jax.ShapeDtypeStruct((1, ROWS, 64), F32),
        ),
        in_specs=[sm, vm, vm, vm, vm, pl.BlockSpec(memory_space=pl.ANY)],
        out_specs=(vm, vm),
        scratch_shapes=[
            pltpu.VMEM((CHUNKS, GROUP, WIDE), BF),
            pltpu.VMEM((2, 8, 2, ROWS, HD), BF),
            pltpu.VMEM((96, GROUP), BF),
            pltpu.VMEM((CHUNKS, 2, ROWS, WIDE), BF),
            pltpu.VMEM((CHUNKS, 2, ROWS, WIDE), BF),
            pltpu.VMEM((CHUNKS, ROWS, WIDE), BF),
            pltpu.VMEM((CHUNKS, ROWS, WIDE), BF),
            pltpu.SemaphoreType.DMA((CHUNKS,)),
            pltpu.SemaphoreType.DMA,
            pltpu.SemaphoreType.DMA,
            pltpu.SemaphoreType.DMA,
            pltpu.SemaphoreType.DMA((CHUNKS,)),
            pltpu.SemaphoreType.DMA((CHUNKS,)),
            pltpu.SemaphoreType.DMA((CHUNKS,)),
            pltpu.SemaphoreType.DMA((CHUNKS,)),
        ],
        compiler_params=pltpu.CompilerParams(
            collective_id=1, has_side_effects=True, vmem_limit_bytes=48 * 2**20
        ),
        name="project",
    )(noise_level, o, stream, latent, w_velocity.T, w_out)


def on_device(
    queries, keys, values, stream, latent, w_out, w_velocity, noise_level, valid_len, span_mask
):
    q, kv = gather(queries, keys, values)
    o = attention(span_mask, valid_len, q, kv)
    return project(noise_level, o, stream, latent, w_velocity, w_out)


def solution(mesh):
    rows = P("span", ("blk", "head"), None)
    return jax.shard_map(
        on_device,
        mesh=mesh,
        in_specs=(rows, rows, rows, rows, rows, P("head", None), P(), P(), P(), P()),
        out_specs=(rows, rows),
        check_vma=False,
    )
```

time: 715 us -> 85.4 us (0.12)
  the two profiles are of different devices: /device:TPU:25 before, /device:TPU:17 now
where the time goes in v1:
time: 85.4 us; the launch traced here: 85 us
  Pallas kernels  75.5 us (88%)
  local copies, waits for them, and re-layouts  8.87 us (10%)
    pallas_call x1, Pallas kernels, gather(): pl.pallas_call(gather_kernel, out_shape=(jax.ShapeDtypeStruct((BLKS, 2, R...  34 us
    pallas_call x1, Pallas kernels, project(): pl.pallas_call(project_kernel, out_shape=(jax.ShapeDtypeStruct((1, ROWS,...  29.1 us
    pallas_call x1, Pallas kernels, attention(): pl.pallas_call(attend_kernel, out_shape=jax.ShapeDtypeStruct((BLKS, 2, RO...  12.4 us
    unnamed x20, local copies, waits for them, and re-layouts  8.87 us

profile of v1, /device:TPU:17, one launch (start us, length us, event | category | flops | bytes accessed | tf_op | source)
XLA Modules:
  0.0 85.0 jit_solution(835417261703844642)
XLA Ops:
  0.6 0.0 copy-start.2
  0.6 0.9 %copy-done.2 = bf16[1,24,4096]{2,1,0:T(8,128)(2,1)S(1)} copy-done((bf16[1,24,4096]{2,1,0:T(8,128)(2,1)S(1)}, bf16[1,24,4096]{2,1,0:T(8,128)(2,1)}, u32[]{:S(2)}) %copy-start.2) | copy-done | bytes 196632
  1.6 0.0 copy-start.3
  1.6 0.9 %copy-done.3 = bf16[1,24,4096]{2,1,0:T(8,128)(2,1)S(1)} copy-done((bf16[1,24,4096]{2,1,0:T(8,128)(2,1)S(1)}, bf16[1,24,4096]{2,1,0:T(8,128)(2,1)}, u32[]{:S(2)}) %copy-start.3) | copy-done | bytes 196632
  2.5 0.0 copy-start.4
  2.5 0.9 %copy-done.4 = bf16[1,24,4096]{2,1,0:T(8,128)(2,1)S(1)} copy-done((bf16[1,24,4096]{2,1,0:T(8,128)(2,1)S(1)}, bf16[1,24,4096]{2,1,0:T(8,128)(2,1)}, u32[]{:S(2)}) %copy-start.4) | copy-done | bytes 196632
  3.4 34.0 %gather.1 = (bf16[16,2,24,128]{3,2,1,0:T(8,128)(2,1)S(1)}, bf16[4,2,16,2,2,24,128]{6,5,4,3,2,1,0:T(8,128)(2,1)S(1)}) custom-call(bf16[1,24,4096]{2,1,0:T(8,128)(2,1)S(1)} %copy-done.2, bf16[1,24,4096]{2,1,0:T(8,128)(2,1)S(1)} %copy-done.3, bf16[1,24,4096]{2,1,0:T(8,128)(2,1)S(1)} %copy-done.4), custom_call_target="tpu_custom_call" | custom-call | tf_op jit(solution)/shard_map/gather/pallas_call | solution.py:207
  37.4 0.0 copy-start.6
  37.4 0.7 copy-done.6
  38.1 0.0 copy-start.7
  38.1 0.7 copy-done.7
  38.7 12.4 %attend.1.o_ref = bf16[16,2,24,128]{3,2,1,0:T(8,128)(2,1)S(1)} custom-call(s32[4,4]{1,0:T(4,128)S(1)} %copy-done.6, s32[4]{0:T(128)S(1)} %copy-done.7, bf16[16,2,24,128]{3,2,1,0:T(8,128)(2,1)S(1)} %get-tuple-element.4.q_ref, bf16[4,2,16,2,2,24,128]{6,5,4,3,2,1,0:T(8,128)(2,1)S(1)} %get-tuple-element.5.kv_ref), custom_call_target="tpu_custom_call" | custom-call | tf_op jit(solution)/shard_map/attend/pallas_call | solution.py:285
  51.2 0.0 copy-start
  51.2 1.1 %copy-done = bf16[6144,64]{0,1:T(8,128)(2,1)S(1)} copy-done((bf16[6144,64]{0,1:T(8,128)(2,1)S(1)}, bf16[6144,64]{0,1:T(8,128)(2,1)}, u32[]{:S(2)}) %copy-start) | copy-done | bytes 786456
  52.3 0.0 copy-start.1
  52.3 1.0 %copy-done.1 = bf16[1,24,6144]{2,1,0:T(8,128)(2,1)S(1)} copy-done((bf16[1,24,6144]{2,1,0:T(8,128)(2,1)S(1)}, bf16[1,24,6144]{2,1,0:T(8,128)(2,1)}, u32[]{:S(2)}) %copy-start.1) | copy-done | bytes 294936
  53.3 0.0 copy-start.5
  53.3 0.7 copy-done.5
  54.0 0.0 copy-start.8
  54.0 0.7 copy-done.8
  54.6 29.1 %project.1 = (bf16[1,24,6144]{2,1,0:T(8,128)(2,1)S(1)}, f32[1,24,64]{2,1,0:T(8,128)S(1)}) custom-call(s32[4]{0:T(128)S(1)} %copy-done.8, bf16[16,2,24,128]{3,2,1,0:T(8,128)(2,1)S(1)} %attend.1.o_ref, bf16[1,24,6144]{2,1,0:T(8,128)(2,1)S(1)} %copy-done.1, f32[1,24,64]{2,1,0:T(8,128)S(1)} %copy-done.5, bf16[64,6144]{1,0:T(8,128)(2,1)S(1)} %bitcast.1, ...), custom_call_target="tpu_custom_call" | custom-call | tf_op jit(solution)/shard_map/project/pallas_call | solution.py:418
  83.7 0.7 copy.14
  84.4 0.6 copy.15
Async XLA Ops:
  0.6 0.9 %copy-start.2 = (bf16[1,24,4096]{2,1,0:T(8,128)(2,1)S(1)}, bf16[1,24,4096]{2,1,0:T(8,128)(2,1)}, u32[]{:S(2)}) copy-start(bf16[1,24,4096]{2,1,0:T(8,128)(2,1)} %q_ref.1) | copy-start | bytes 589828
  1.6 0.9 %copy-start.3 = (bf16[1,24,4096]{2,1,0:T(8,128)(2,1)S(1)}, bf16[1,24,4096]{2,1,0:T(8,128)(2,1)}, u32[]{:S(2)}) copy-start(bf16[1,24,4096]{2,1,0:T(8,128)(2,1)} %k_ref.1) | copy-start | bytes 589828
  2.5 0.9 %copy-start.4 = (bf16[1,24,4096]{2,1,0:T(8,128)(2,1)S(1)}, bf16[1,24,4096]{2,1,0:T(8,128)(2,1)}, u32[]{:S(2)}) copy-start(bf16[1,24,4096]{2,1,0:T(8,128)(2,1)} %v_ref.1) | copy-start | bytes 589828
  37.4 0.7 copy-start.6
  38.1 0.7 copy-start.7
  51.2 1.1 %copy-start = (bf16[6144,64]{0,1:T(8,128)(2,1)S(1)}, bf16[6144,64]{0,1:T(8,128)(2,1)}, u32[]{:S(2)}) copy-start(bf16[6144,64]{0,1:T(8,128)(2,1)} %param.16) | copy-start | bytes 2359300
  52.3 1.0 %copy-start.1 = (bf16[1,24,6144]{2,1,0:T(8,128)(2,1)S(1)}, bf16[1,24,6144]{2,1,0:T(8,128)(2,1)}, u32[]{:S(2)}) copy-start(bf16[1,24,6144]{2,1,0:T(8,128)(2,1)} %stream_ref.1) | copy-start | bytes 884740
  53.3 0.7 copy-start.5
  54.0 0.7 copy-start.8

commit v2 on v0

v2 whole, which is shorter than its diff:
```python
import jax
import jax.numpy as jnp
from jax import lax
from jax.experimental import pallas as pl
from jax.experimental.pallas import tpu as pltpu
from jax.sharding import PartitionSpec as P

HD = 128
LEVELS = 8
SPANS = 4
BLKS = 16
ROWS = 24
HEADS = 32
SLOTS = 32
TOK = SLOTS * ROWS
MODEL = 6144
GROUP = 1024
CHUNKS = 6
WIDE = MODEL // CHUNKS
LOG_SCALE = HD ** -0.5 * 1.4426950408889634
TILE = 256
DEPTHS = (4, 0, 3, 7, 5, 1, 2, 6)
NEG = -1e30
MESH = pl.DeviceIdType.MESH
BF = jnp.bfloat16
F32 = jnp.float32


def place():
    span = lax.axis_index("span")
    blk = lax.axis_index("blk")
    head = lax.axis_index("head")
    return span, blk, lax.div(head, 2), lax.rem(head, 2)


def flip(blk):
    return blk + 1 - 2 * lax.rem(blk, 2)


def block_kernel(
    noise_ref, valid_ref, mask_ref, q_hbm, k_hbm, v_hbm, stream_hbm, latent_hbm, wv_hbm, w_hbm, out_ref, next_ref,
    q_in, k_in, v_in, stream_in, latent_in, wv_in, w_buf, q_got, kv_got, qx, kx, vx, acc, best, base, o_flat, o_buf,
    heads, lhs, near_out, near_in, far_out, far_in,
    in_sem, w_sem, a_send, a_recv, a_own, y_send, y_recv, c_send, c_recv, h_send, h_recv, h_own,
    n_send, n_recv, f_send, f_recv,
):
    span, blk, half, core = place()
    mine = half * BLKS + blk
    depth = lax.div(blk, 2)
    column = half * 2 + lax.rem(blk, 2)
    sibling = {"head": half * 2 + 1 - core}
    partner = {"blk": flip(blk), "head": (1 - half) * 2 + core}
    barrier = pltpu.get_barrier_semaphore()

    def greet(i, carry):
        other = lax.rem(mine + i, HEADS)
        pl.semaphore_signal(
            barrier, inc=1, device_id={"blk": lax.rem(other, BLKS), "head": lax.div(other, BLKS) * 2 + core},
            device_id_type=MESH,
        )
        return carry

    def greet_other(i, carry):
        pl.semaphore_signal(
            barrier, inc=1, device_id={"blk": lax.rem(blk + i, BLKS), "head": half * 2 + 1 - core}, device_id_type=MESH
        )
        return carry

    lax.fori_loop(1, HEADS, greet, 0)
    lax.fori_loop(0, BLKS, greet_other, 0)
    for i in range(1, SPANS):
        pl.semaphore_signal(barrier, inc=1, device_id={"span": lax.rem(span + i, SPANS)}, device_id_type=MESH)

    fetch = [
        pltpu.make_async_copy(src, dst, in_sem.at[i])
        for i, (src, dst) in enumerate(
            ((k_hbm, k_in), (v_hbm, v_in), (q_hbm, q_in), (stream_hbm, stream_in), (latent_hbm, latent_in), (wv_hbm, wv_in))
        )
    ]
    for copy in fetch:
        copy.start()
    loads = [
        pltpu.make_async_copy(w_hbm.at[:, pl.ds(n * WIDE, WIDE)], w_buf.at[n], w_sem.at[n]) for n in range(CHUNKS)
    ]
    lane = lax.broadcasted_iota(jnp.int32, (TOK, HD), 1)
    first = lane == 0
    row = lax.broadcasted_iota(jnp.int32, (TOK, HD), 0)
    turn = lax.div(row, ROWS)
    dz = jnp.zeros_like(turn)
    for step in range(8):
        dz = jnp.where(lax.div(turn, 4) == step, DEPTHS[step], dz)
    z = lax.rem(depth + 8 - dz, 8)
    x = lax.rem(column + 4 - lax.rem(turn, 4), 4)
    base[...] = (z * 2 + lax.rem(x, 2)) * (4 * ROWS) + lax.div(x, 2) * (2 * ROWS) + lax.rem(row, ROWS)
    unit = jnp.where(first, 1.0, 0.0).astype(BF)
    qx[:, HD:] = unit
    acc[...] = jnp.zeros_like(acc)
    best[...] = jnp.full_like(best, NEG)

    def prepare(c2, carry):
        limit = valid_ref[c2] * mask_ref[span, c2]
        for rel in range(2):
            here = pl.ds(rel * TOK, TOK)
            vx[c2, here, HD:] = unit
            pos = base[...] + lax.rem(core + rel, 2) * ROWS
            kx[c2, here, HD:] = jnp.where(first & (pos >= limit), NEG, 0.0).astype(BF)
        return carry

    lax.fori_loop(0, span + 1, prepare, 0)
    for i in range(3):
        fetch[i].wait()
    pl.semaphore_wait(barrier, HEADS - 1 + BLKS + SPANS - 1)

    def cols(head):
        return pl.ds(pl.multiple_of(head * HD, HD), HD)

    def target(dz, dx):
        z = lax.rem(depth + dz, 8)
        x = lax.rem(column + dx, 4)
        there = lax.div(x, 2)
        to = z * 2 + lax.rem(x, 2)
        return there * BLKS + to, {"blk": to, "head": there * 2 + core}, there

    own = [
        pltpu.make_async_copy(k_in.at[0, :, cols(mine)], kv_got.at[span, 0, 0, 0, 4], a_own.at[0]),
        pltpu.make_async_copy(v_in.at[0, :, cols(mine)], kv_got.at[span, 0, 0, 1, 4], a_own.at[1]),
        pltpu.make_async_copy(q_in.at[0, :, cols(mine)], q_got.at[BLKS + blk], a_own.at[2]),
    ]
    for step, dz in enumerate(DEPTHS):
        j, s = step // 2, step % 2 * 4

        def send_kv(dx, carry, dz=dz, j=j, s=s):
            other, device, there = target(dz, dx)
            for t, src in enumerate((k_in, v_in)):
                pltpu.make_async_remote_copy(
                    src.at[0, :, cols(other)], kv_got.at[span, 0, j, t, s + dx], a_send.at[t], a_recv.at[j],
                    device_id=device, device_id_type=MESH,
                ).start()
            return carry

        lax.fori_loop(0 if dz else 1, 4, send_kv, 0)
    for copy in own:
        copy.start()
    for dz in DEPTHS:

        def send_q(dx, carry, dz=dz):
            other, device, there = target(dz, dx)
            cross = lax.rem(half + there, 2)
            slot = (1 - cross) * BLKS + blk + cross * (1 - 2 * lax.rem(blk, 2))
            pltpu.make_async_remote_copy(
                q_in.at[0, :, cols(other)], q_got.at[slot], a_send.at[2], a_recv.at[4],
                device_id=device, device_id_type=MESH,
            ).start()
            return carry

        lax.fori_loop(0 if dz else 1, 4, send_q, 0)
    for load in loads:
        load.start()
    own[0].wait()
    own[1].wait()

    def arrived(j):
        count = 8 if j else 7
        whole = kv_got.at[0, 0, 0, :, pl.ds(0, count)]
        pltpu.make_async_copy(whole, whole, a_recv.at[j]).wait()

    def along(c2, j, to, which):
        return pltpu.make_async_remote_copy(
            kv_got.at[c2, 0, j], kv_got.at[c2, 0, j], y_send.at[which], y_recv.at[c2, j],
            device_id={"span": to}, device_id_type=MESH,
        )

    def beside(c2, j):
        return pltpu.make_async_remote_copy(
            kv_got.at[c2, 0, j], kv_got.at[c2, 1, j], c_send.at[c2, j], c_recv.at[c2, j],
            device_id=sibling, device_id_type=MESH,
        )

    plans = (
        "A0>1,3;A1>1,3;A2>1,3;R11>3;A3>1,3,2",
        "A0>2;A1>0,2;R00>2;A2>2;R01;A3>2,3",
        "A0>3;A1>3;R10>3;A2>3;R00;R01;A3>3;R11;R12>3",
        "A0;A1;R01>2;A2;R20;R00;R10;R21;R02>2;A3;R11;R22",
    )
    later = ("", "R02;R03", "R02;R13;R03", "R12;R23;R03;R13")

    def play(c, plan, count=0):
        sends, over = [], []
        for event in plan.split(";") if plan else ():
            what, _, to = event.partition(">")
            if what[0] == "A":
                c2, j = c, int(what[1])
                arrived(j)
            else:
                c2, j = int(what[1]), int(what[2])
                along(c2, j, 0, 0).wait_recv()
            for t in to.split(",") if to else ():
                copy = along(c2, j, int(t), count + len(sends))
                copy.start()
                sends.append(copy)
            if c2 <= c:
                copy = beside(c2, j)
                copy.start()
                over.append(copy)
        return sends, over

    for c in range(SPANS):

        @pl.when(span == c)
        def _(c=c):
            sends, over = play(c, plans[c])
            for copy in sends:
                copy.wait_send()
            for copy in over:
                copy.wait_send()

    own[2].wait()
    others = q_got.at[pl.ds(0, HEADS - 1)]
    pltpu.make_async_copy(others, others, a_recv.at[4]).wait()
    qx[:, :HD] = q_got[...].reshape(TOK, HD)

    goal = lax.div(blk, 8)
    rel = lax.rem(goal + core, 2)
    place_in = lax.rem(blk, 8)
    keep = goal == core

    def compute(c2, finish):
        for j in range(4):
            beside(c2, j).wait_recv()
        for r in range(2):
            here = pl.ds(r * TOK, TOK)
            kx[c2, here, :HD] = kv_got[c2, r, :, 0].reshape(TOK, HD)
            vx[c2, here, :HD] = kv_got[c2, r, :, 1].reshape(TOK, HD)
        for t in range(TOK // TILE):
            rows = slice(t * TILE, (t + 1) * TILE)
            scores = lax.dot_general(
                qx[rows], kx[c2], (((1,), (1,)), ((), ())), preferred_element_type=F32
            )
            old = best[rows]
            fresh = jnp.maximum(old, jnp.max(scores, axis=1, keepdims=True))
            unnorm = jnp.exp2(scores * LOG_SCALE - (fresh * LOG_SCALE)[:, :1]).astype(BF)
            part = jnp.dot(unnorm, vx[c2], preferred_element_type=F32)
            total = acc[rows] * jnp.exp2((old - fresh) * LOG_SCALE)[:, :1] + part
            if finish:
                o_flat[rows] = (total[:, :HD] / total[:, HD : HD + 1]).astype(BF)
                if t:
                    send_part(t - 1)
            else:
                acc[rows] = total
                best[rows] = fresh

    def send_part(part):
        here = pl.ds(part * BLKS, BLKS)
        o_buf[here] = o_flat[part * BLKS * ROWS : (part + 1) * BLKS * ROWS].reshape(BLKS, ROWS, HD)

        def send_o(i, carry):
            other = lax.rem(blk + i, BLKS)
            pltpu.make_async_remote_copy(
                o_buf.at[part * BLKS + other], heads.at[part, rel, place_in], h_send.at[part], h_recv.at[part],
                device_id={"blk": other, "head": half * 2 + goal}, device_id_type=MESH,
            ).start()
            return carry

        lax.fori_loop(1, BLKS, send_o, 0)

        @pl.when(keep)
        def _():
            pltpu.make_async_copy(
                o_buf.at[part * BLKS + blk], heads.at[part, rel, place_in], h_own.at[part]
            ).start()

        @pl.when(jnp.logical_not(keep))
        def _():
            send_o(0, 0)

    def wait_part(part):
        most, every = o_buf.at[pl.ds(0, BLKS - 1)], o_buf.at[pl.ds(0, BLKS)]

        @pl.when(keep)
        def _():
            pltpu.make_async_copy(
                o_buf.at[part * BLKS + blk], heads.at[part, rel, place_in], h_own.at[part]
            ).wait()
            pltpu.make_async_copy(most, most, h_recv.at[part]).wait()
            pltpu.make_async_copy(most, most, h_send.at[part]).wait()

        @pl.when(jnp.logical_not(keep))
        def _():
            pltpu.make_async_copy(every, every, h_recv.at[part]).wait()
            pltpu.make_async_copy(every, every, h_send.at[part]).wait()

        for r in range(2):
            for j in range(8):
                lhs[part, r * ROWS : (r + 1) * ROWS, j * HD : (j + 1) * HD] = heads[part, r, j]

    def one_span(i, carry):
        compute(span - i, False)
        for c in range(1, SPANS):

            @pl.when((span == c) & (i == 0))
            def _(c=c):
                sends, over = play(c, later[c])
                for copy in over:
                    copy.wait_send()

        return carry

    lax.fori_loop(0, span, one_span, 0)
    compute(0, True)

    def near(part, n):
        return pltpu.make_async_remote_copy(
            near_out.at[part, n], near_in.at[part, n], n_send.at[part, n], n_recv.at[part, n],
            device_id=sibling, device_id_type=MESH,
        )

    def far(n):
        return pltpu.make_async_remote_copy(
            far_out.at[n], far_in.at[n], f_send.at[n], f_recv.at[n], device_id=partner, device_id_type=MESH
        )

    wait_part(0)
    held = [None] * CHUNKS
    for n in range(CHUNKS + 1):
        if n < CHUNKS:
            loads[n].wait()
            part = jnp.dot(lhs[0], w_buf[n], preferred_element_type=F32)
            near_out[0, n] = part[ROWS:].astype(BF)
            near(0, n).start()
            held[n] = part[:ROWS]
        m = n - 1
        if 0 <= m < CHUNKS:
            near(0, m).wait_recv()
            far_out[m] = (held[m] + near_in[0, m].astype(F32)).astype(BF)
            far(m).start()
    wait_part(1)
    for n in range(CHUNKS):
        part = jnp.dot(lhs[1], w_buf[n], preferred_element_type=F32)
        near_out[1, n] = part[ROWS:].astype(BF)
        near(1, n).start()
        held[n] = part[:ROWS]
    for i in range(3, 6):
        fetch[i].wait()
    velocity = jnp.zeros((ROWS, 64), F32)
    for m in range(CHUNKS):
        near(1, m).wait_recv()
        far(m).wait_recv()
        here = slice(m * WIDE, (m + 1) * WIDE)
        update = held[m] + near_in[1, m].astype(F32) + far_in[m].astype(F32)
        fresh = (stream_in[0, :, here].astype(F32) + update).astype(BF)
        out_ref[0, :, here] = fresh
        velocity += lax.dot_general(
            fresh, wv_in[:, here], (((1,), (1,)), ((), ())), preferred_element_type=F32
        )
    level = jnp.full((ROWS, 64), noise_ref[span], jnp.int32).astype(F32)

    def sigma(value):
        u = 1.0 - value / LEVELS
        return 3.0 * u / (1.0 + 2.0 * u)

    next_ref[0] = latent_in[0] + (sigma(level + 1.0) - sigma(level)) * velocity
    for t in range(3):
        pltpu.make_async_copy(others, others, a_send.at[t]).wait()
    for n in range(CHUNKS):
        near(0, n).wait_send()
        near(1, n).wait_send()
        far(n).wait_send()


def finish_kernel(rows_in, next_in, rows_out, next_out, rows_buf, next_buf, in_sem, out_sem):
    wide = MODEL // 4
    first, second = [], []
    for n in range(4):
        here = (slice(None), slice(None), pl.ds(n * wide, wide))
        first.append(pltpu.make_async_copy(rows_in.at[here], rows_buf.at[here], in_sem.at[n]))
        second.append(pltpu.make_async_copy(rows_buf.at[here], rows_out.at[here], out_sem.at[n]))
    first.append(pltpu.make_async_copy(next_in, next_buf, in_sem.at[4]))
    second.append(pltpu.make_async_copy(next_buf, next_out, out_sem.at[4]))
    for copy in first:
        copy.start()
    for one, two in zip(first, second):
        one.wait()
        two.start()
    for copy in second:
        copy.wait()


def on_device(
    queries, keys, values, stream, latent, w_out, w_velocity, noise_level, valid_len, span_mask
):
    anywhere = pl.BlockSpec(memory_space=pl.ANY)
    sm = pl.BlockSpec(memory_space=pltpu.SMEM)
    vm = pl.BlockSpec(memory_space=pltpu.VMEM)
    dma = pltpu.SemaphoreType.DMA
    rows, following = pl.pallas_call(
        block_kernel,
        out_shape=(
            jax.ShapeDtypeStruct((1, ROWS, MODEL), BF),
            jax.ShapeDtypeStruct((1, ROWS, 64), F32),
        ),
        in_specs=[sm] * 3 + [anywhere] * 7,
        out_specs=(vm, vm),
        scratch_shapes=[
            pltpu.VMEM((1, ROWS, HEADS * HD), BF),
            pltpu.VMEM((1, ROWS, HEADS * HD), BF),
            pltpu.VMEM((1, ROWS, HEADS * HD), BF),
            pltpu.VMEM((1, ROWS, MODEL), BF),
            pltpu.VMEM((1, ROWS, 64), F32),
            pltpu.VMEM((64, MODEL), BF),
            pltpu.VMEM((CHUNKS, GROUP, WIDE), BF),
            pltpu.VMEM((SLOTS, ROWS, HD), BF),
            pltpu.VMEM((SPANS, 2, 4, 2, 8, ROWS, HD), BF),
            pltpu.VMEM((TOK, 2 * HD), BF),
            pltpu.VMEM((SPANS, 2 * TOK, 2 * HD), BF),
            pltpu.VMEM((SPANS, 2 * TOK, 2 * HD), BF),
            pltpu.VMEM((TOK, 2 * HD), F32),
            pltpu.VMEM((TOK, HD), F32),
            pltpu.VMEM((TOK, HD), jnp.int32),
            pltpu.VMEM((TOK, HD), BF),
            pltpu.VMEM((SLOTS, ROWS, HD), BF),
            pltpu.VMEM((2, 2, 8, ROWS, HD), BF),
            pltpu.VMEM((2, 2 * ROWS, GROUP), BF),
            pltpu.VMEM((2, CHUNKS, ROWS, WIDE), BF),
            pltpu.VMEM((2, CHUNKS, ROWS, WIDE), BF),
            pltpu.VMEM((CHUNKS, ROWS, WIDE), BF),
            pltpu.VMEM((CHUNKS, ROWS, WIDE), BF),
            dma((6,)),
            dma((CHUNKS,)),
            dma((3,)),
            dma((5,)),
            dma((3,)),
            dma((10,)),
            dma((4, 4)),
            dma((4, 4)),
            dma((4, 4)),
            dma((2,)),
            dma((2,)),
            dma((2,)),
            dma((2, CHUNKS)),
            dma((2, CHUNKS)),
            dma((CHUNKS,)),
            dma((CHUNKS,)),
        ],
        compiler_params=pltpu.CompilerParams(
            collective_id=0, has_side_effects=True, vmem_limit_bytes=58 * 2**20
        ),
        name="block",
    )(noise_level, valid_len, span_mask, queries, keys, values, stream, latent, w_velocity.T, w_out)
    return pl.pallas_call(
        finish_kernel,
        out_shape=(
            jax.ShapeDtypeStruct((1, ROWS, MODEL), BF),
            jax.ShapeDtypeStruct((1, ROWS, 64), F32),
        ),
        in_specs=[anywhere] * 2,
        out_specs=(anywhere, anywhere),
        scratch_shapes=[
            pltpu.VMEM((1, ROWS, MODEL), BF),
            pltpu.VMEM((1, ROWS, 64), F32),
            dma((5,)),
            dma((5,)),
        ],
        compiler_params=pltpu.CompilerParams(vmem_limit_bytes=58 * 2**20),
        name="finish",
    )(rows, following)


def solution(mesh):
    rows = P("span", ("blk", "head"), None)
    return jax.shard_map(
        on_device,
        mesh=mesh,
        in_specs=(rows, rows, rows, rows, rows, P("head", None), P(), P(), P(), P()),
        out_specs=(rows, rows),
        check_vma=False,
    )
```

time: 715 us -> 62 us (0.09); the launches traced: 707 us -> 61.9 us
  waiting for transfers between devices: 453 us -> 0 us
  other arithmetic: 83.9 us -> 0 us
  Pallas kernels: 0 us -> 61.2 us
  local copies, waits for them, and re-layouts: 59.3 us -> 0 us
  blocking collectives: 51 us -> 0 us
  matrix products: 37.4 us -> 0 us
  between operations: 15.6 us -> 0.64 us
    all_gather x2 -> x0, waiting for transfers between devices: 402 us -> none  [the longest x1 245 us: on_device(): lax.all_gather(every_v, 'blk', axis=1, tiled=True)]
    unnamed x3 -> x0, other arithmetic: 70.4 us -> none
    pallas_call x0 -> x2, Pallas kernels: none -> 61.2 us  [the longest x1 59.5 us: on_device(): pl.pallas_call(block_kernel, out_shape=(jax.ShapeDtypeStruct((1, ROWS, MO...]
    unnamed x27 -> x0, local copies, waits for them, and re-layouts: 51 us -> none
    reduce_scatter x1 -> x0, waiting for transfers between devices: 38.4 us -> none  [on_device(): lax.psum_scatter(jnp.dot(attn, w_out, preferred_element_type=jnp.float32)...]
    dot_general x4 -> x0, matrix products: 37.4 us -> none  [the longest x1 14.1 us: attend(): jnp.einsum('hqk,khd->hqd', unnorm.astype(jnp.bfloat16), val_heads, prefer...]
    all_to_all x2 -> x0, blocking collectives: 27.2 us -> none  [the longest x1 16.3 us: on_device(): lax.all_to_all(values, 'head', split_axis=2, concat_axis=1, tiled=True)]
    all_gather x2 -> x0, blocking collectives: 23.8 us -> none  [the longest x1 12.7 us: on_device(): lax.all_gather(mine_v, 'span', axis=0, tiled=True)]
  transfers between devices with their start and end apart: 4 -> 0, of which waited for: 4 -> 0; matrix products, arithmetic and copies ran while one was open for 13% -> 0% of each run, Pallas kernels for 0% -> 0%
where the time goes in v2:
time: 62 us; the launch traced here: 61.9 us
  Pallas kernels  61.2 us (99%)
  between operations  0.64 us (1%)
    pallas_call x1, Pallas kernels, on_device(): pl.pallas_call(block_kernel, out_shape=(jax.ShapeDtypeStruct((1, ROWS, MO...  59.5 us
    pallas_call x1, Pallas kernels, on_device(): pl.pallas_call(finish_kernel, out_shape=(jax.ShapeDtypeStruct((1, ROWS, M...  1.72 us

profile of v2, /device:TPU:25, one launch (start us, length us, event | category | flops | bytes accessed | tf_op | source)
XLA Modules:
  0.0 61.9 jit_solution(3046076689351207724)
XLA Ops:
  0.6 59.5 %block.1 = (bf16[1,24,6144]{2,1,0:T(8,128)(2,1)}, f32[1,24,64]{2,1,0:T(8,128)}) custom-call(s32[4]{0:T(128)} %noise_ref.1, s32[4]{0:T(128)} %valid_ref.1, s32[4,4]{1,0:T(4,128)} %mask_ref.1, bf16[1,24,4096]{2,1,0:T(8,128)(2,1)} %q_hbm.1, bf16[1,24,4096]{2,1,0:T(8,128)(2,1)} %k_hbm.1, bf16[1,24,4096]{2,1,0:T(8,128)(2,1)} %v_hbm.1, ...), custom_call_target="tpu_custom_call" | custom-call | tf_op jit(solution)/shard_map/block/pallas_call | solution.py:395
  60.2 1.7 %finish.1 = (bf16[1,24,6144]{2,1,0:T(8,128)(2,1)}, f32[1,24,64]{2,1,0:T(8,128)}) custom-call(bf16[1,24,6144]{2,1,0:T(8,128)(2,1)} %get-tuple-element.4.rows_in, f32[1,24,64]{2,1,0:T(8,128)} %get-tuple-element.5.next_in), custom_call_target="tpu_custom_call" | custom-call | tf_op jit(solution)/shard_map/finish/pallas_call | solution.py:449

commit v3 on v2

--- a/solution.py
+++ b/solution.py
@@ -19,7 +19,8 @@
 WIDE = MODEL // CHUNKS
 LOG_SCALE = HD ** -0.5 * 1.4426950408889634
 TILE = 256
-DEPTHS = (4, 0, 3, 7, 5, 1, 2, 6)
+DEPTHS = (0, 1, 7, 2, 6, 3, 5, 4)
+HOME = DEPTHS.index(0)
 NEG = -1e30
 MESH = pl.DeviceIdType.MESH
 BF = jnp.bfloat16
@@ -122,8 +123,8 @@
         return there * BLKS + to, {"blk": to, "head": there * 2 + core}, there
 
     own = [
-        pltpu.make_async_copy(k_in.at[0, :, cols(mine)], kv_got.at[span, 0, 0, 0, 4], a_own.at[0]),
-        pltpu.make_async_copy(v_in.at[0, :, cols(mine)], kv_got.at[span, 0, 0, 1, 4], a_own.at[1]),
+        pltpu.make_async_copy(k_in.at[0, :, cols(mine)], kv_got.at[span, 0, HOME // 2, 0, HOME % 2 * 4], a_own.at[0]),
+        pltpu.make_async_copy(v_in.at[0, :, cols(mine)], kv_got.at[span, 0, HOME // 2, 1, HOME % 2 * 4], a_own.at[1]),
         pltpu.make_async_copy(q_in.at[0, :, cols(mine)], q_got.at[BLKS + blk], a_own.at[2]),
     ]
     for step, dz in enumerate(DEPTHS):
@@ -160,7 +161,7 @@
     own[1].wait()
 
     def arrived(j):
-        count = 8 if j else 7
+        count = 7 if j == HOME // 2 else 8
         whole = kv_got.at[0, 0, 0, :, pl.ds(0, count)]
         pltpu.make_async_copy(whole, whole, a_recv.at[j]).wait()
 
@@ -177,15 +178,16 @@
         )
 
     plans = (
-        "A0>1,3;A1>1,3;A2>1,3;R11>3;A3>1,3,2",
-        "A0>2;A1>0,2;R00>2;A2>2;R01;A3>2,3",
-        "A0>3;A1>3;R10>3;A2>3;R00;R01;A3>3;R11;R12>3",
-        "A0;A1;R01>2;A2;R20;R00;R10;R21;R02>2;A3;R11;R22",
+        "A0>1,3;A1>1,3;R11>3;A2>1,3,2;A3>1,3,2",
+        "A0>2;A1>0,2;R00>2;A2>2,3;A3>2,3",
+        "A0>3;A1>3;R10>3;A2>3;R00;A3>3",
+        "A0;A1;R01>2;A2;R20;R00;R10;A3",
     )
-    later = ("", "R02;R03", "R02;R13;R03", "R12;R23;R03;R13")
-
-    def play(c, plan, count=0):
-        sends, over = [], []
+    later = (("", ""), ("R01;R02;R03", ""), ("R11;R12;R13;R01", "R02;R03"), ("R21;R22;R23;R11", "R02;R03;R12;R13"))
+    started = [([], []) for _ in range(SPANS)]
+
+    def play(c, plan):
+        sends, over = started[c]
         for event in plan.split(";") if plan else ():
             what, _, to = event.partition(">")
             if what[0] == "A":
@@ -195,24 +197,29 @@
                 c2, j = int(what[1]), int(what[2])
                 along(c2, j, 0, 0).wait_recv()
             for t in to.split(",") if to else ():
-                copy = along(c2, j, int(t), count + len(sends))
-                copy.start()
-                sends.append(copy)
+                sends.append((c2, j, int(t), len(sends)))
+                along(*sends[-1]).start()
             if c2 <= c:
-                copy = beside(c2, j)
-                copy.start()
-                over.append(copy)
-        return sends, over
+                over.append((c2, j))
+                beside(c2, j).start()
+
+    def settle():
+        for c in range(SPANS):
+
+            @pl.when(span == c)
+            def _(c=c):
+                sends, over = started[c]
+                for what in sends:
+                    along(*what).wait_send()
+                for what in over:
+                    beside(*what).wait_send()
+
 
     for c in range(SPANS):
 
         @pl.when(span == c)
         def _(c=c):
-            sends, over = play(c, plans[c])
-            for copy in sends:
-                copy.wait_send()
-            for copy in over:
-                copy.wait_send()
+            play(c, plans[c])
 
     own[2].wait()
     others = q_got.at[pl.ds(0, HEADS - 1)]
@@ -253,15 +260,16 @@
         here = pl.ds(part * BLKS, BLKS)
         o_buf[here] = o_flat[part * BLKS * ROWS : (part + 1) * BLKS * ROWS].reshape(BLKS, ROWS, HD)
 
-        def send_o(i, carry):
-            other = lax.rem(blk + i, BLKS)
+        def send_o(other):
             pltpu.make_async_remote_copy(
                 o_buf.at[part * BLKS + other], heads.at[part, rel, place_in], h_send.at[part], h_recv.at[part],
                 device_id={"blk": other, "head": half * 2 + goal}, device_id_type=MESH,
             ).start()
-            return carry
-
-        lax.fori_loop(1, BLKS, send_o, 0)
+
+        for dz in DEPTHS:
+            for dx in range(2):
+                if dz or dx:
+                    send_o(lax.rem(depth + dz, 8) * 2 + lax.rem(blk + dx, 2))
 
         @pl.when(keep)
         def _():
@@ -271,7 +279,7 @@
 
         @pl.when(jnp.logical_not(keep))
         def _():
-            send_o(0, 0)
+            send_o(blk)
 
     def wait_part(part):
         most, every = o_buf.at[pl.ds(0, BLKS - 1)], o_buf.at[pl.ds(0, BLKS)]
@@ -296,12 +304,12 @@
     def one_span(i, carry):
         compute(span - i, False)
         for c in range(1, SPANS):
-
-            @pl.when((span == c) & (i == 0))
-            def _(c=c):
-                sends, over = play(c, later[c])
-                for copy in over:
-                    copy.wait_send()
+            for turn, plan in enumerate(later[c]):
+                if plan:
+
+                    @pl.when((span == c) & (i == turn))
+                    def _(c=c, plan=plan):
+                        play(c, plan)
 
         return carry
 
@@ -359,6 +367,7 @@
         return 3.0 * u / (1.0 + 2.0 * u)
 
     next_ref[0] = latent_in[0] + (sigma(level + 1.0) - sigma(level)) * velocity
+    settle()
     for t in range(3):
         pltpu.make_async_copy(others, others, a_send.at[t]).wait()
     for n in range(CHUNKS):
@@ -429,7 +438,7 @@
             dma((3,)),
             dma((5,)),
             dma((3,)),
-            dma((10,)),
+            dma((12,)),
             dma((4, 4)),
             dma((4, 4)),
             dma((4, 4)),

time: 62 us -> 60.9 us (0.982)
  Pallas kernels: 61.2 us -> 59.7 us
    pallas_call x1, Pallas kernels: 59.5 us -> 58 us  [on_device(): pl.pallas_call(block_kernel, out_shape=(jax.ShapeDtypeStruct((1, ROWS, MO...]
where the time goes in v3:
time: 60.9 us; the launch traced here: 60.3 us
  Pallas kernels  59.7 us (98%)
  between operations  0.64 us (1%)
    pallas_call x1, Pallas kernels, on_device(): pl.pallas_call(block_kernel, out_shape=(jax.ShapeDtypeStruct((1, ROWS, MO...  58 us
    pallas_call x1, Pallas kernels, on_device(): pl.pallas_call(finish_kernel, out_shape=(jax.ShapeDtypeStruct((1, ROWS, M...  1.72 us

profile of v3, /device:TPU:25, one launch (start us, length us, event | category | flops | bytes accessed | tf_op | source)
XLA Modules:
  0.0 60.3 jit_solution(14637044096586689534)
XLA Ops:
  0.6 58.0 %block.1 = (bf16[1,24,6144]{2,1,0:T(8,128)(2,1)}, f32[1,24,64]{2,1,0:T(8,128)}) custom-call(s32[4]{0:T(128)} %noise_ref.1, s32[4]{0:T(128)} %valid_ref.1, s32[4,4]{1,0:T(4,128)} %mask_ref.1, bf16[1,24,4096]{2,1,0:T(8,128)(2,1)} %q_hbm.1, bf16[1,24,4096]{2,1,0:T(8,128)(2,1)} %k_hbm.1, bf16[1,24,4096]{2,1,0:T(8,128)(2,1)} %v_hbm.1, ...), custom_call_target="tpu_custom_call" | custom-call | tf_op jit(solution)/shard_map/block/pallas_call | solution.py:404
  58.6 1.7 %finish.1 = (bf16[1,24,6144]{2,1,0:T(8,128)(2,1)}, f32[1,24,64]{2,1,0:T(8,128)}) custom-call(bf16[1,24,6144]{2,1,0:T(8,128)(2,1)} %get-tuple-element.4.rows_in, f32[1,24,64]{2,1,0:T(8,128)} %get-tuple-element.5.next_in), custom_call_target="tpu_custom_call" | custom-call | tf_op jit(solution)/shard_map/finish/pallas_call | solution.py:458

commit v4 on v3

--- a/solution.py
+++ b/solution.py
@@ -178,12 +178,12 @@
         )
 
     plans = (
-        "A0>1,3;A1>1,3;R11>3;A2>1,3,2;A3>1,3,2",
-        "A0>2;A1>0,2;R00>2;A2>2,3;A3>2,3",
-        "A0>3;A1>3;R10>3;A2>3;R00;A3>3",
-        "A0;A1;R01>2;A2;R20;R00;R10;A3",
+        "A0>3,1;A1>3,1;R11>3;A2>3,2,1;A3>3,2,1",
+        "A0>2;A1>0,2;A2>3,2;A3>3,2",
+        "A0>3;A1>3;R10>3;A2>3;A3>3",
+        "A0;R00>2;A1;R01>2;A2;R20;R10;A3",
     )
-    later = (("", ""), ("R01;R02;R03", ""), ("R11;R12;R13;R01", "R02;R03"), ("R21;R22;R23;R11", "R02;R03;R12;R13"))
+    later = (("", ""), ("R00;R01;R02;R03", ""), ("R11;R12;R13;R00;R01", "R02;R03"), ("R21;R22;R23;R11", "R02;R03;R12;R13"))
     started = [([], []) for _ in range(SPANS)]
 
     def play(c, plan):

time: 60.9 us -> 60.4 us (level)
  no operation moved by 1% of the time
where the time goes in v4:
time: 60.4 us; the launch traced here: 60.2 us
  Pallas kernels  59.6 us (99%)
  between operations  0.64 us (1%)
    pallas_call x1, Pallas kernels, on_device(): pl.pallas_call(block_kernel, out_shape=(jax.ShapeDtypeStruct((1, ROWS, MO...  57.8 us
    pallas_call x1, Pallas kernels, on_device(): pl.pallas_call(finish_kernel, out_shape=(jax.ShapeDtypeStruct((1, ROWS, M...  1.72 us

profile of v4, /device:TPU:25, one launch (start us, length us, event | category | flops | bytes accessed | tf_op | source)
XLA Modules:
  0.0 60.2 jit_solution(17192504447640882549)
XLA Ops:
  0.6 57.8 %block.1 = (bf16[1,24,6144]{2,1,0:T(8,128)(2,1)}, f32[1,24,64]{2,1,0:T(8,128)}) custom-call(s32[4]{0:T(128)} %noise_ref.1, s32[4]{0:T(128)} %valid_ref.1, s32[4,4]{1,0:T(4,128)} %mask_ref.1, bf16[1,24,4096]{2,1,0:T(8,128)(2,1)} %q_hbm.1, bf16[1,24,4096]{2,1,0:T(8,128)(2,1)} %k_hbm.1, bf16[1,24,4096]{2,1,0:T(8,128)(2,1)} %v_hbm.1, ...), custom_call_target="tpu_custom_call" | custom-call | tf_op jit(solution)/shard_map/block/pallas_call | solution.py:404
  58.5 1.7 %finish.1 = (bf16[1,24,6144]{2,1,0:T(8,128)(2,1)}, f32[1,24,64]{2,1,0:T(8,128)}) custom-call(bf16[1,24,6144]{2,1,0:T(8,128)(2,1)} %get-tuple-element.4.rows_in, f32[1,24,64]{2,1,0:T(8,128)} %get-tuple-element.5.next_in), custom_call_target="tpu_custom_call" | custom-call | tf_op jit(solution)/shard_map/finish/pallas_call | solution.py:458

commit v5 on v4

--- a/solution.py
+++ b/solution.py
@@ -221,6 +221,16 @@
         def _(c=c):
             play(c, plans[c])
 
+    def pack(c2):
+        for r in range(2):
+            if r:
+                for j in range(4):
+                    beside(c2, j).wait_recv()
+            here = pl.ds(r * TOK, TOK)
+            kx[c2, here, :HD] = kv_got[c2, r, :, 0].reshape(TOK, HD)
+            vx[c2, here, :HD] = kv_got[c2, r, :, 1].reshape(TOK, HD)
+
+    pack(span)
     own[2].wait()
     others = q_got.at[pl.ds(0, HEADS - 1)]
     pltpu.make_async_copy(others, others, a_recv.at[4]).wait()
@@ -232,12 +242,6 @@
     keep = goal == core
 
     def compute(c2, finish):
-        for j in range(4):
-            beside(c2, j).wait_recv()
-        for r in range(2):
-            here = pl.ds(r * TOK, TOK)
-            kx[c2, here, :HD] = kv_got[c2, r, :, 0].reshape(TOK, HD)
-            vx[c2, here, :HD] = kv_got[c2, r, :, 1].reshape(TOK, HD)
         for t in range(TOK // TILE):
             rows = slice(t * TILE, (t + 1) * TILE)
             scores = lax.dot_general(
@@ -311,6 +315,7 @@
                     def _(c=c, plan=plan):
                         play(c, plan)
 
+        pack(span - i - 1)
         return carry
 
     lax.fori_loop(0, span, one_span, 0)

time: 60.4 us -> 60.9 us (level)
  no operation moved by 1% of the time
where the time goes in v5:
time: 60.9 us; the launch traced here: 60.7 us
  Pallas kernels  60 us (99%)
  between operations  0.64 us (1%)
    pallas_call x1, Pallas kernels, on_device(): pl.pallas_call(block_kernel, out_shape=(jax.ShapeDtypeStruct((1, ROWS, MO...  58.3 us
    pallas_call x1, Pallas kernels, on_device(): pl.pallas_call(finish_kernel, out_shape=(jax.ShapeDtypeStruct((1, ROWS, M...  1.72 us

profile of v5, /device:TPU:25, one launch (start us, length us, event | category | flops | bytes accessed | tf_op | source)
XLA Modules:
  0.0 60.7 jit_solution(9223899094654269105)
XLA Ops:
  0.6 58.3 %block.1 = (bf16[1,24,6144]{2,1,0:T(8,128)(2,1)}, f32[1,24,64]{2,1,0:T(8,128)}) custom-call(s32[4]{0:T(128)} %noise_ref.1, s32[4]{0:T(128)} %valid_ref.1, s32[4,4]{1,0:T(4,128)} %mask_ref.1, bf16[1,24,4096]{2,1,0:T(8,128)(2,1)} %q_hbm.1, bf16[1,24,4096]{2,1,0:T(8,128)(2,1)} %k_hbm.1, bf16[1,24,4096]{2,1,0:T(8,128)(2,1)} %v_hbm.1, ...), custom_call_target="tpu_custom_call" | custom-call | tf_op jit(solution)/shard_map/block/pallas_call | solution.py:409
  59.0 1.7 %finish.1 = (bf16[1,24,6144]{2,1,0:T(8,128)(2,1)}, f32[1,24,64]{2,1,0:T(8,128)}) custom-call(bf16[1,24,6144]{2,1,0:T(8,128)(2,1)} %get-tuple-element.4.rows_in, f32[1,24,64]{2,1,0:T(8,128)} %get-tuple-element.5.next_in), custom_call_target="tpu_custom_call" | custom-call | tf_op jit(solution)/shard_map/finish/pallas_call | solution.py:463
